TPU v7x, 128 devices: a whole 4x4x4 slice. The times are simulated.
128 devices in a mesh: dp: 32 (over x, z, core), help: 4 (over y).
Axes of the slice: x: 4, y: 4, z: 4, core: 2. Of those that a mesh axis runs over, the one named last changes fastest.
Arguments:
- embeddings: bfloat16 [131072, 1024], P(('dp', 'help')), may hold values from -1600 to 1600
- clusters: int32 [131072], P(('dp', 'help')), may hold values from 0 to 63, as said below
- doc_order: int32 [131072], P(('dp', 'help')), may hold values from 0 to 131071, each once
Outputs:
- similarity: float32 [131072], P(('dp', 'help'))
Inputs may be any that keep to these rules, and one draw needn't show every extreme that they name: `clusters`: among the 1024 documents of one device no cluster appears more than 32 times; one cluster appears exactly 32 times on every device. `doc_order`: every number from 0 to 131071 appears once.
All inputs are finite; a program needn't handle non-finite values.
Results may differ from a plain program's by a relative error of at most 0.00033.
Values may be sent and summed in bfloat16 or wider, within the bound.
A program may use at most 128 MiB of HBM per device.

v0:
```python
import jax
import jax.numpy as jnp
from jax import lax
from jax.sharding import PartitionSpec as P

CL_DEV = 2


def whitening(gram_total, col_sum, doc_count, feature_count):
    center = col_sum / doc_count
    spread = gram_total / doc_count - center[:, None] * center[None, :]
    ridge_term = 0.001 * jnp.trace(spread) / feature_count
    identity = jnp.eye(feature_count, dtype=jnp.float32)
    factor = jnp.linalg.cholesky(spread + ridge_term * identity)
    inverse = lax.linalg.triangular_solve(factor, identity, left_side=True, lower=True)
    return (center, inverse)


def whiten(source_rows, center, inverse):
    shifted = lax.dot_general(
        center[None, :],
        inverse,
        (((1,), (1,)), ((), ())),
        precision=lax.Precision.HIGHEST,
        preferred_element_type=jnp.float32,
    )
    raw_rows = source_rows.astype(jnp.float32)
    projected = (
        lax.dot_general(
            raw_rows,
            inverse,
            (((1,), (1,)), ((), ())),
            precision=lax.Precision.HIGH,
            preferred_element_type=jnp.float32,
        )
        - shifted
    )
    row_scale = lax.rsqrt(jnp.sum(projected * projected, axis=1, keepdims=True) + 1e-06)
    return (projected * row_scale).astype(jnp.bfloat16)


def row_best(queries, query_order, key_rows, key_order):
    scores = jnp.einsum("nqd,nkd->nqk", queries, key_rows, preferred_element_type=jnp.float32)
    earlier = key_order[:, None, :] < query_order[:, :, None]
    return jnp.max(jnp.where(earlier, scores, -jnp.inf), axis=2)


def per_device(embeddings, clusters, doc_order):
    row_count = embeddings.shape[0]
    feature_count = embeddings.shape[1]
    owner_count = lax.axis_size("dp")
    helper_count = lax.axis_size("help")
    doc_count = row_count * owner_count * helper_count
    held_count = CL_DEV
    cluster_count = held_count * owner_count
    slot_cap = 2 * row_count // cluster_count
    span_slots = owner_count * slot_cap
    col_part = jnp.sum(embeddings, axis=0, dtype=jnp.float32)
    gram_part = lax.dot_general(
        embeddings, embeddings, (((0,), (0,)), ((), ())), preferred_element_type=jnp.float32
    )
    gram_total, col_sum = lax.psum((gram_part, col_part), ("dp", "help"))
    center, inverse = whitening(gram_total, col_sum, doc_count, feature_count)
    labels = jnp.arange(cluster_count, dtype=jnp.int32)
    member = clusters[:, None] == labels[None, :]
    row_numbers = jnp.arange(row_count, dtype=jnp.int32)
    before = (row_numbers[None, :] < row_numbers[:, None]).astype(jnp.bfloat16)
    earlier_count = jnp.dot(before, member.astype(jnp.bfloat16), preferred_element_type=jnp.float32)
    slot_index = jnp.sum(jnp.where(member, earlier_count, 0.0), axis=1).astype(jnp.int32)
    target = clusters % held_count * span_slots + clusters // held_count * slot_cap + slot_index
    payload = whiten(embeddings, center, inverse)
    outgoing = (
        jnp.zeros((held_count * span_slots, feature_count), jnp.bfloat16)
        .at[target]
        .set(payload, unique_indices=True)
    )
    outgoing_order = (
        jnp.full((held_count * span_slots,), doc_count, jnp.int32)
        .at[target]
        .set(doc_order, unique_indices=True)
    )
    outgoing = outgoing.reshape(held_count, span_slots, feature_count)
    outgoing_order = outgoing_order.reshape(held_count, span_slots)
    received = lax.all_to_all(outgoing, "dp", split_axis=1, concat_axis=1, tiled=True)
    received_order = lax.all_to_all(outgoing_order, "dp", split_axis=1, concat_axis=1, tiled=True)
    running = jnp.full(received_order.shape, -1.0, jnp.float32)
    key_rows = lax.all_gather(received, "help", axis=1, tiled=True)
    key_order = lax.all_gather(received_order, "help", axis=1, tiled=True)
    best_prior = jnp.maximum(running, row_best(received, received_order, key_rows, key_order))
    returned = lax.all_to_all(best_prior, "dp", split_axis=1, concat_axis=1, tiled=True)
    similarity = returned.reshape(-1)[target]
    return similarity


def solution(mesh):
    in_specs = (P(("dp", "help"), None), P(("dp", "help")), P(("dp", "help")))
    out_specs = P(("dp", "help"))
    return jax.shard_map(
        per_device, mesh=mesh, in_specs=in_specs, out_specs=out_specs, check_vma=False
    )
```

profile of v0, /device:TPU:1, one launch (start us, length us, event | category | flops | bytes accessed | tf_op | source)
XLA Modules:
  0.0 849.5 jit_solution(10617502917893588577)
XLA Ops:
  15.1 69.5 %psum.15 = f32[1024]{0:T(1024)S(1)} all-reduce(f32[1024]{0:T(1024)S(1)} %convert_reduce_fusion), channel_id=1, replica_groups=mesh['dp'=32,'help'=4] {'dp','help'}, use_global_device_ids=true, to_apply=%region_4.5 | all-reduce | flops 1024 | bytes 8192 | tf_op jit(solution)/shard_map/psum | solution.py:62
  89.5 81.7 %all-reduce.3.cloned.1.call-done = f32[1024,1024]{0,1:T(8,128)} async-done(((f32[1024,1024]{0,1:T(8,128)}), f32[1024,1024]{0,1:T(8,128)}) %all-reduce.3.cloned.1.call-update) | async-done | bytes 4194320 | tf_op jit(solution)/shard_map/psum | solution.py:62
  191.5 11.7 %cholesky.222 = f32[128,128]{1,0:T(8,128)S(1)} custom-call(f32[128,128]{1,0:T(8,128)S(1)} %cholesky.577), custom_call_target="Cholesky" | custom-call | tf_op jit(solution)/shard_map/jit(cholesky)/cholesky | solution.py:14
  203.2 9.8 %custom-call.62 = f32[1,128,128]{1,2,0:T(8,128)S(1)} custom-call(f32[1,128,128]{2,1,0:T(8,128)S(1)} %get-tuple-element.79), custom_call_target="InvertDiagBlocksLowerTriangular" | custom-call | tf_op jit(solution)/shard_map/jit(cholesky)/cholesky | solution.py:14
  216.1 11.7 %cholesky.243 = f32[128,128]{1,0:T(8,128)S(1)} custom-call(f32[128,128]{1,0:T(8,128)S(1)} %cholesky.581), custom_call_target="Cholesky" | custom-call | tf_op jit(solution)/shard_map/jit(cholesky)/cholesky | solution.py:14
  230.1 10.7 %custom-call.63 = f32[1,128,128]{1,2,0:T(8,128)S(1)} custom-call(f32[1,128,128]{2,1,0:T(8,128)} %get-tuple-element.77), custom_call_target="InvertDiagBlocksLowerTriangular" | custom-call | tf_op jit(solution)/shard_map/jit(cholesky)/cholesky | solution.py:14
  246.3 11.7 %cholesky.466 = f32[128,128]{1,0:T(8,128)S(1)} custom-call(f32[128,128]{1,0:T(8,128)S(1)} %cholesky.586), custom_call_target="Cholesky" | custom-call | tf_op jit(solution)/shard_map/jit(cholesky)/cholesky | solution.py:14
  273.2 11.7 %cholesky.485 = f32[128,128]{1,0:T(8,128)S(1)} custom-call(f32[128,128]{1,0:T(8,128)S(1)} %cholesky.591), custom_call_target="Cholesky" | custom-call | tf_op jit(solution)/shard_map/jit(cholesky)/cholesky | solution.py:14
  285.7 9.8 %custom-call.65 = f32[1,128,128]{1,2,0:T(8,128)S(1)} custom-call(f32[1,128,128]{2,1,0:T(8,128)S(1)} %get-tuple-element.73), custom_call_target="InvertDiagBlocksLowerTriangular" | custom-call | tf_op jit(solution)/shard_map/jit(cholesky)/cholesky | solution.py:14
  299.8 12.2 %cholesky.504 = f32[128,128]{1,0:T(8,128)S(1)} custom-call(f32[128,128]{1,0:T(8,128)S(1)} %cholesky.596), custom_call_target="Cholesky" | custom-call | tf_op jit(solution)/shard_map/jit(cholesky)/cholesky | solution.py:14
  312.8 9.8 %custom-call.66 = f32[1,128,128]{1,2,0:T(8,128)S(1)} custom-call(f32[1,128,128]{2,1,0:T(8,128)S(1)} %get-tuple-element.71), custom_call_target="InvertDiagBlocksLowerTriangular" | custom-call | tf_op jit(solution)/shard_map/jit(cholesky)/cholesky | solution.py:14
  326.9 11.7 %cholesky.524 = f32[128,128]{1,0:T(8,128)S(1)} custom-call(f32[128,128]{1,0:T(8,128)S(1)} %cholesky.601), custom_call_target="Cholesky" | custom-call | tf_op jit(solution)/shard_map/jit(cholesky)/cholesky | solution.py:14
  353.0 11.9 %cholesky.544 = f32[128,128]{1,0:T(8,128)S(1)} custom-call(f32[128,128]{1,0:T(8,128)S(1)} %cholesky.606), custom_call_target="Cholesky" | custom-call | tf_op jit(solution)/shard_map/jit(cholesky)/cholesky | solution.py:14
  365.6 9.8 %custom-call.68 = f32[1,128,128]{1,2,0:T(8,128)S(1)} custom-call(f32[1,128,128]{2,1,0:T(8,128)S(1)} %get-tuple-element.67), custom_call_target="InvertDiagBlocksLowerTriangular" | custom-call | tf_op jit(solution)/shard_map/jit(cholesky)/cholesky | solution.py:14
  378.6 11.7 %cholesky.562 = f32[128,128]{1,0:T(8,128)S(1)} custom-call(f32[128,128]{1,0:T(8,128)S(1)} %convolution_subtract_fusion.11), custom_call_target="Cholesky" | custom-call | tf_op jit(solution)/shard_map/jit(cholesky)/cholesky | solution.py:14
  405.8 28.1 %while.1 = (s32[]{:T(128)}, f32[1024,1024]{0,1:T(8,128)}, s32[8,2]{0,1:T(2,128)S(1)}, f32[8,128,128]{2,1,0:T(8,128)}, s32[]{:T(128)}) while((s32[]{:T(128)}, f32[1024,1024]{0,1:T(8,128)}, s32[8,2]{0,1:T(2,128)S(1)}, f32[8,128,128]{2,1,0:T(8,128)}, s32[]{:T(128)}) %tuple.55), condition=%wide.while_cond, body=%wide.while_body.sunk | while | flops 2 | bytes 393829 | solution.py:15
  433.9 79.8 %custom-call.69 = f32[8,128,128]{1,2,0:T(8,128)S(1)} custom-call(f32[8,128,128]{2,1,0:T(8,128)} %get-tuple-element.12), custom_call_target="InvertDiagBlocksLowerTriangular" | custom-call | tf_op jit(solution)/shard_map/triangular_solve | solution.py:15
  579.0 56.8 %all_to_all.23 = bf16[2,1024,1024]{2,0,1:T(2,128)(2,1)S(1)} all-to-all(bf16[2,1024,1024]{2,0,1:T(2,128)(2,1)S(1)} %copy.99), channel_id=1, replica_groups=mesh['dp'=32,'help'=4] {'dp'}, dimensions={1} | all-to-all | bytes 8388608 | tf_op jit(solution)/shard_map/all_to_all | solution.py:84
  645.7 11.0 %all_to_all.24 = s32[2,32,32]{2,0,1:T(2,128)S(1)} all-to-all(s32[2,32,32]{2,0,1:T(2,128)S(1)} %copy.71), channel_id=1, replica_groups=mesh['dp'=32,'help'=4] {'dp'}, dimensions={1} | all-to-all | bytes 16384 | tf_op jit(solution)/shard_map/all_to_all | solution.py:85
  656.8 10.2 %all_gather.6 = s32[2,4096]{1,0:T(2,128)S(1)} all-gather(s32[2,1024]{1,0:T(2,128)S(1)} %all_to_all.17), channel_id=1, replica_groups=mesh['dp'=32,'help'=4] {'help'}, dimensions={1}, use_global_device_ids=true | all-gather | bytes 40960 | tf_op jit(solution)/shard_map/all_gather | solution.py:88
  666.9 124.7 %all-gather.2.cloned.1.call-done = bf16[2,4096,1024]{2,1,0:T(8,128)(2,1)} async-done(((bf16[2,1024,1024]{2,1,0:T(8,128)(2,1)}), bf16[2,4096,1024]{2,1,0:T(8,128)(2,1)}) %all-gather.2.cloned.1.call-update) | async-done | bytes 16777232 | tf_op jit(solution)/shard_map/all_gather | solution.py:87
  791.6 25.4 %select_reduce_fusion = f32[2,1024]{1,0:T(2,128)S(1)} fusion(s32[2,1024]{1,0:T(2,128)S(1)} %all_to_all.17, s32[2,4096]{1,0:T(2,128)S(1)} %all_gather.6, bf16[2,4096,1024]{2,1,0:T(8,128)(2,1)} %all-gather.2.cloned.1.call-done, bf16[2,1024,1024]{2,0,1:T(2,128)(2,1)} %copy-done.1), kind=kOutput, calls=%fused_computation.5 | convolution fusion | flops 17205032960 | bytes 21020672 | tf_op jit(solution)/shard_map/nqd,nkd->nqk/dot_general | solution.py:43
  817.1 14.7 %all_to_all.25 = f32[2,32,32]{2,0,1:T(2,128)S(1)} all-to-all(f32[2,32,32]{2,0,1:T(2,128)S(1)} %copy.102), channel_id=1, replica_groups=mesh['dp'=32,'help'=4] {'dp'}, dimensions={1} | all-to-all | bytes 16384 | tf_op jit(solution)/shard_map/all_to_all | solution.py:90
  831.9 10.5 %gather_fusion = f32[1024]{0:T(1024)} fusion(f32[2048]{0:T(1024)S(1)} %reshape.100, s32[1024]{0:T(1024)S(1)} %get-tuple-element.37), kind=kCustom, calls=%fused_computation | custom fusion | bytes 12288 | tf_op jit(solution)/shard_map/gather | solution.py:91
  (166 shorter events, 201.1 us)
Async XLA Ops:
  6.5 164.6 %all-reduce.3.cloned.1.call-start = ((), (), s32[]{:S(2)}) async-start(), calls=%async_computation.3 | async-start | bytes 8388608 | tf_op jit(solution)/shard_map/psum | solution.py:62
  13.1 1.6 copy-start.4
  13.1 72.0 %copy-start.6 = (s32[1024]{0:T(1024)S(1)}, s32[1024]{0:T(1024)}, u32[]{:S(2)}) copy-start(s32[1024]{0:T(1024)} %param.4) | copy-start | bytes 12292
  13.1 778.5 %all-gather.2.cloned.1.call-start = ((), (), s32[]{:S(2)}) async-start(), calls=%async_computation.4 | async-start | bytes 20971520 | tf_op jit(solution)/shard_map/all_gather | solution.py:87
  189.5 2.0 copy-start.3
  230.0 11.4 %copy-start.5 = (f32[128,128]{0,1:T(8,128)S(1)}, f32[128,128]{0,1:T(8,128)}, u32[]{:S(2)}) copy-start(f32[128,128]{0,1:T(8,128)} %copy.77) | copy-start | bytes 196612
  241.9 2.0 copy-start
  296.6 98.5 %copy-start.7 = (f32[128]{0:T(128)S(1)}, f32[128]{0:T(128)}, u32[]{:S(2)}) copy-start(f32[128]{0:T(128)} %get-tuple-element.76) | copy-start | bytes 1540
  400.9 4.9 copy-start.8
  513.7 4.4 copy-start.2
  635.9 1.9 copy-start.1
Sparse Core Ops, SparseCore 0:
  13.3 157.8 all-reduce.2
  641.2 150.3 all-gather.1
where the time goes:
time: 856 us; the launch traced here: 849 us
  other arithmetic  272 us (32%)
  waiting for transfers between devices  206 us (24%)
  blocking collectives  162 us (19%)
  matrix products  105 us (12%)
  local copies, waits for them, and re-layouts  83.9 us (10%)
  between operations  19.8 us (2%)
    another operation x30, other arithmetic, whitening(): factor = jnp.linalg.cholesky(spread + ridge_term * identity)  170 us
    all_gather x1, waiting for transfers between devices, per_device(): key_rows = lax.all_gather(received, 'help', axis=1, tiled=True)  125 us
    another operation x3, other arithmetic, whitening(): lax.linalg.triangular_solve(factor, identity, left_side=True, lower=True)  85.2 us
    psum x1, waiting for transfers between devices, per_device(): gram_total, col_sum = lax.psum((gram_part, col_part), ('dp', 'help'))  81.7 us
    psum x1, blocking collectives, per_device(): gram_total, col_sum = lax.psum((gram_part, col_part), ('dp', 'help'))  69.5 us
    all_to_all x1, blocking collectives, per_device(): lax.all_to_all(outgoing, 'dp', split_axis=1, concat_axis=1, tiled=True)  56.8 us
    another operation x15, matrix products, whitening(): lax.linalg.triangular_solve(factor, identity, left_side=True, lower=True)  38.5 us
    another operation x40, local copies, waits for them, and re-layouts  28 us
  transfers between devices with their start and end apart: 2, of which 2 were waited for; matrix products, arithmetic and copies ran while one was open for 1% of the time, Pallas kernels for 0%

commit v1 on v0

v1 whole, which is shorter than its diff:
```python
import jax
import jax.numpy as jnp
from jax import lax
from jax.experimental import pallas as pl
from jax.experimental.pallas import tpu as pltpu
from jax.sharding import PartitionSpec as P

F32 = jnp.float32
BF = jnp.bfloat16
MESH = pl.DeviceIdType.MESH
BL = 128
SEND = 32
CHIPS = 64
DIGITS = 128
AXES = ("x", "y", "z")


def dot(a, b, ca, cb):
    return lax.dot_general(a, b, (((ca,), (cb,)), ((), ())), preferred_element_type=F32)


def dot_full(a, b, ca, cb):
    return lax.dot_general(
        a,
        b,
        (((ca,), (cb,)), ((), ())),
        precision=lax.Precision.HIGHEST,
        preferred_element_type=F32,
    )


def bcast(v):
    return jnp.broadcast_to(v, (8, BL))


def sum_tree(x):
    while len(x) > 1:
        x = [x[i] + x[i + 1] for i in range(0, len(x), 2)]
    return x[0]


def chol_inverse_block(rows):
    sub = lax.broadcasted_iota(jnp.int32, (8, BL), 0)
    lane = lax.broadcasted_iota(jnp.int32, (8, BL), 1)
    unit = [jnp.where(lane == sub + 8 * i, 1.0, 0.0).astype(F32) for i in range(16)]
    rows = list(rows)
    out = []
    for p in range(16):
        r, t = rows[p], unit[p]
        tf = t
        cols = [bcast(r[:, 8 * p + k : 8 * p + k + 1]) for k in range(8)]
        scale = jnp.zeros((8, BL), F32)
        for j in range(8):
            d = bcast(cols[j][j : j + 1])
            inv = 1.0 / d
            pick = sub == j
            scale = jnp.where(pick, d, scale)
            cj = cols[j]
            tf = tf - jnp.where(sub > j, cj, 0.0) * (bcast(tf[j : j + 1]) * inv)
            for k in range(j + 1, 8):
                row = bcast(cols[k][j : j + 1]) * inv
                cols[k] = jnp.where(pick, row, cols[k] - cj * row)
            row = bcast(r[j : j + 1]) * inv
            r = jnp.where(pick, row, r - cj * row)
            row = bcast(t[j : j + 1]) * inv
            t = jnp.where(pick, row, t - cj * row)
        out.append(tf * lax.rsqrt(scale))
        for i in range(p + 1, 16):
            m = [bcast(rows[i][:, 8 * p + k : 8 * p + k + 1]) for k in range(8)]
            rows[i] = rows[i] - sum_tree([m[k] * bcast(r[k : k + 1]) for k in range(8)])
            unit[i] = unit[i] - sum_tree([m[k] * bcast(t[k : k + 1]) for k in range(8)])
    return out


def factor(m_ref, w_ref):
    blocks = m_ref.shape[0] // BL

    def step(p, _):
        off = pl.multiple_of(p * BL, BL)
        here = pl.ds(off, BL)
        out = chol_inverse_block([m_ref[pl.ds(off + 8 * i, 8), here] for i in range(16)])
        for i in range(16):
            w_ref[8 * i : 8 * i + 8, :] = out[i]
        w = w_ref[...]
        m_ref[here, :] = dot_full(w, m_ref[here, :], 1, 0)
        m_ref[here, here] = w

        def trail(i, _):
            there = pl.ds(pl.multiple_of(i * BL, BL), BL)
            g = m_ref[here, there]
            m_ref[there, here] = jnp.zeros((BL, BL), F32)
            m_ref[there, :] = m_ref[there, :] - dot_full(g, m_ref[here, :], 0, 0)
            return 0

        lax.fori_loop(p + 1, blocks, trail, 0)
        return 0

    lax.fori_loop(0, blocks, step, 0)


def place(i):
    return min(i, 7 - i) * BL, 0 if i < 4 else (i + 1) * BL


def slots_of(clusters_row):
    n = clusters_row.shape[1]
    member = lax.broadcasted_iota(jnp.int32, (CHIPS, n), 0) == clusters_row
    before = lax.broadcasted_iota(jnp.int32, (n, n), 0) < lax.broadcasted_iota(jnp.int32, (n, n), 1)
    count = dot(member.astype(F32).astype(BF), before.astype(F32).astype(BF), 1, 0)
    slot = jnp.sum(jnp.where(member, count, 0.0), axis=0, keepdims=True)
    return member, slot.astype(jnp.int32)


def digits_of(order_row, doc_count):
    n = order_row.shape[1]
    value = doc_count - order_row
    row = lax.broadcasted_iota(jnp.int32, (DIGITS, n), 0)
    d = jnp.where(row == 0, value >> 16, jnp.where(row == 1, (value >> 8) & 255, value & 255))
    return jnp.where(row < 3, d, 0).astype(F32).T.astype(BF)


def kernel(
    doc_count,
    emb_ref,
    clusters_ref,
    order_ref,
    out_ref,
    emb,
    outgoing,
    received,
    keys,
    packed,
    half_in,
    acc,
    in1,
    sum1,
    in2,
    in3,
    total,
    mat,
    w_block,
    w_hi,
    w_lo,
    key_rank,
    ret_out,
    ret_in,
    emb_sem,
    core_send,
    core_recv,
    ring_send,
    ring_recv,
    up_send,
    up_recv,
    out_send,
    out_recv,
    pair_send,
    pair_recv,
    ret_send,
    ret_recv,
):
    dp = lax.axis_index("dp")
    y = lax.axis_index("help")
    core = dp % 2
    x = dp // 8
    z = (dp // 2) % 4
    chip = (dp // 2) * 4 + y
    sibling = (dp + 1 - 2 * core, y)
    rows = emb.shape[0]
    width = emb.shape[1]

    def chip_device(c):
        return ((c // 4) * 2 + core, c % 4)

    def axis_peer(axis, d):
        if axis == "x":
            to = (x + d) % 4
            return ((to * 4 + z) * 2 + core, y), to
        if axis == "z":
            to = (z + d) % 4
            return ((x * 4 + to) * 2 + core, y), to
        to = (y + d) % 4
        return (dp, to), to

    place_on = {"x": x, "y": y, "z": z}

    barrier = pltpu.get_barrier_semaphore()

    def greet(d, _):
        pl.semaphore_signal(
            barrier, inc=1, device_id=chip_device((chip + d) % CHIPS), device_id_type=MESH
        )
        return 0

    lax.fori_loop(1, CHIPS, greet, 0)
    pl.semaphore_signal(barrier, inc=1, device_id=sibling, device_id_type=MESH)
    load = pltpu.make_async_copy(emb_ref, emb, emb_sem)
    load.start()
    member, slot = slots_of(clusters_ref[...])
    target = clusters_ref[...] * SEND + slot
    digits = digits_of(order_ref[...], doc_count)
    load.wait()

    col_sum = dot(jnp.ones((8, rows), BF), emb[...], 1, 0)
    sub = lax.broadcasted_iota(jnp.int32, (BL, BL), 0)
    lane = lax.broadcasted_iota(jnp.int32, (BL, BL), 1)
    for b in range(width // 256):
        block = dot(emb[:, 256 * b : 256 * b + 256], emb[:, 256 * b :], 0, 0)
        for i in (2 * b, 2 * b + 1):
            r0, c0 = place(i)
            skip = (i - 2 * b) * BL
            part = block[skip : skip + BL, skip:]
            w = part.shape[1]
            packed[r0 : r0 + BL, c0 : c0 + w] = part
            cs = jnp.broadcast_to(col_sum[0:1, i * BL : i * BL + BL], (BL, BL))
            spare = jnp.where(sub == BL - 2, cs, pltpu.roll(cs, 64, 1))
            use = (sub >= BL - 2) & (lane < 64)
            packed[r0 : r0 + BL, c0 : c0 + BL] = jnp.where(use, spare, part[:, :BL])

    pl.semaphore_wait(barrier, CHIPS)

    half = packed.shape[0] // 2
    mine = pl.ds(pl.multiple_of(core * half, 8), half)
    other = pl.ds(pl.multiple_of((1 - core) * half, 8), half)
    swap = pltpu.make_async_remote_copy(
        src_ref=packed.at[other],
        dst_ref=half_in,
        send_sem=core_send,
        recv_sem=core_recv,
        device_id=sibling,
        device_id_type=MESH,
    )
    swap.start()

    def place_rows(k, _):
        b = (k + chip // 8) % 8
        first = pl.multiple_of(b * 256, 256)
        here = lax.broadcasted_iota(jnp.int32, (256, rows), 0) + first
        pick = (here == target).astype(F32).astype(BF)
        outgoing[pl.ds(first, 256), 0:width] = dot(pick, emb[...], 1, 0).astype(BF)
        outgoing[pl.ds(first, 256), width:] = dot(pick, digits, 1, 0).astype(BF)
        return 0

    lax.fori_loop(0, 8, place_rows, 0)
    swap.wait_recv()
    acc[...] = packed[mine, :] + half_in[...]

    def ring_copy(stage, q, d, src, dst, device):
        return pltpu.make_async_remote_copy(
            src_ref=src,
            dst_ref=dst,
            send_sem=ring_send.at[stage * 9 + q * 3 + d - 1],
            recv_sem=ring_recv.at[stage * 9 + q * 3 + d - 1],
            device_id=device,
            device_id_type=MESH,
        )

    third = acc.shape[1] // 3
    cols = [slice(q * third, (q + 1) * third) for q in range(3)]
    axis_a = [AXES[q] for q in range(3)]
    axis_b = [AXES[(q + 1) % 3] for q in range(3)]
    axis_c = [AXES[(q + 2) % 3] for q in range(3)]
    sent = []
    stage1 = {}
    for d in (2, 1, 3):
        for q in range(3):
            device, to = axis_peer(axis_a[q], d)
            src = acc.at[pl.ds(pl.multiple_of(to * 64, 64), 64), cols[q]]
            c = ring_copy(0, q, d, src, in1.at[q, d - 1], device)
            c.start()
            stage1[q, d] = c
    stage2 = {}
    for q in range(3):
        for d in (1, 3, 2):
            stage1[q, d].wait_recv()
        a = place_on[axis_a[q]]
        own = acc[pl.ds(pl.multiple_of(a * 64, 64), 64), cols[q]]
        sum1[q] = (own + in1[q, 0]) + (in1[q, 1] + in1[q, 2])
        for d in (2, 1, 3):
            device, to = axis_peer(axis_b[q], d)
            src = sum1.at[q, pl.ds(pl.multiple_of(to * 16, 16), 16), :]
            c = ring_copy(1, q, d, src, in2.at[q, d - 1], device)
            c.start()
            stage2[q, d] = c
    stage3 = {}
    for q in range(3):
        for d in (1, 3, 2):
            stage2[q, d].wait_recv()
        b = place_on[axis_b[q]]
        c_at = place_on[axis_c[q]]
        own = sum1[q, pl.ds(pl.multiple_of(b * 16, 16), 16), :]
        in3[q, c_at] = (own + in2[q, 0]) + (in2[q, 1] + in2[q, 2])
        for d in (2, 1, 3):
            device, to = axis_peer(axis_c[q], d)
            c = ring_copy(2, q, d, in3.at[q, c_at], in3.at[q, c_at], device)
            c.start()
            stage3[q, d] = c
    stage4 = {}
    for q in range(3):
        for d in (1, 3, 2):
            stage3[q, d].wait_recv()
        a, b = place_on[axis_a[q]], place_on[axis_b[q]]
        there = pl.ds(pl.multiple_of(core * half + a * 64 + b * 16, 16), 16)
        total[there, cols[q]] = (in3[q, 0] + in3[q, 1]) + (in3[q, 2] + in3[q, 3])
        for d in (2, 1, 3):
            device, to = axis_peer(axis_b[q], d)
            c = ring_copy(3, q, d, total.at[there, cols[q]], total.at[there, cols[q]], device)
            c.start()
            stage4[q, d] = c
    stage5 = {}
    for q in range(3):
        for d in (1, 3, 2):
            stage4[q, d].wait_recv()
        a = place_on[axis_a[q]]
        there = pl.ds(pl.multiple_of(core * half + a * 64, 64), 64)
        for d in (2, 1, 3):
            device, to = axis_peer(axis_a[q], d)
            c = ring_copy(4, q, d, total.at[there, cols[q]], total.at[there, cols[q]], device)
            c.start()
            stage5[q, d] = c
    up = []
    for q in range(3):
        for d in (1, 3, 2):
            stage5[q, d].wait_recv()
        c = pltpu.make_async_remote_copy(
            src_ref=total.at[mine, cols[q]],
            dst_ref=total.at[mine, cols[q]],
            send_sem=up_send.at[q],
            recv_sem=up_recv.at[q],
            device_id=sibling,
            device_id_type=MESH,
        )
        c.start()
        up.append(c)

    def out_copy(to, at, source):
        return pltpu.make_async_remote_copy(
            src_ref=outgoing.at[pl.ds(pl.multiple_of(to * SEND, SEND), SEND), :],
            dst_ref=received.at[pl.ds(pl.multiple_of(source * SEND, SEND), SEND), :],
            send_sem=out_send.at[at],
            recv_sem=out_recv.at[at],
            device_id=chip_device(to),
            device_id_type=MESH,
        )

    def send_out(d, _):
        out_copy((chip + d) % CHIPS, d, chip).start()
        return 0

    lax.fori_loop(1, CHIPS, send_out, 0)
    own_rows = pl.ds(pl.multiple_of(chip * SEND, SEND), SEND)
    received[own_rows, :] = outgoing[own_rows, :]
    for c in up:
        c.wait_recv()

    inv_n = 1.0 / doc_count
    center = []
    trace = jnp.zeros((BL, BL), F32)
    for i in range(8):
        r0, c0 = place(i)
        d = total[r0 : r0 + BL, c0 : c0 + BL]
        tail = d[BL - 8 :, :]
        c = jnp.where(lane[:1] < 64, tail[6:7], pltpu.roll(tail, 64, 1)[7:8]) * inv_n
        center.append(c)
        cb = jnp.broadcast_to(c, (BL, BL))
        trace = trace + jnp.where(lane == sub, d * inv_n - cb * cb, 0.0)
    trace = jnp.sum(jnp.sum(trace, axis=1, keepdims=True), axis=0, keepdims=True)
    ridge = 0.001 * trace * (1.0 / width)
    for i in range(8):
        r0, c0 = place(i)
        col = jnp.broadcast_to(center[i], (BL, BL)).T
        for j in range(i, 8):
            g = total[r0 : r0 + BL, c0 + (j - i) * BL : c0 + (j - i + 1) * BL]
            if j == i:
                g = jnp.where(lane >= sub, g, g.T)
            v = g * inv_n - col * center[j]
            if j == i:
                v = v + jnp.where(lane == sub, ridge, 0.0)
            mat[i * BL : (i + 1) * BL, j * BL : (j + 1) * BL] = v
        for j in range(i):
            mat[i * BL : (i + 1) * BL, j * BL : (j + 1) * BL] = jnp.zeros((BL, BL), F32)
    factor(mat, w_block)
    shift = []
    for j in range(8):
        shift.append(
            dot_full(
                jnp.concatenate([jnp.broadcast_to(c, (8, BL)) for c in center[: j + 1]], axis=1),
                mat[j * BL : (j + 1) * BL, : (j + 1) * BL],
                1,
                1,
            )[0:1]
        )
    shift = jnp.concatenate(shift, axis=1)
    for i in range(8):
        for j in range(8):
            at = (slice(i * BL, (i + 1) * BL), slice(j * BL, (j + 1) * BL))
            if j <= i:
                v = mat[at]
                hi = v.astype(BF)
                w_hi[at] = hi
                w_lo[at] = (v - hi.astype(F32)).astype(BF)
            else:
                w_hi[at] = jnp.zeros((BL, BL), BF)
                w_lo[at] = jnp.zeros((BL, BL), BF)

    def arrive(d, _):
        out_copy((chip + d) % CHIPS, d, chip).wait_recv()
        return 0

    lax.fori_loop(1, CHIPS, arrive, 0)

    keys_half = received.shape[0]
    base = core * keys_half

    def pair_copy(k):
        there = pl.ds(pl.multiple_of(base + k * 256, 256), 256)
        return pltpu.make_async_remote_copy(
            src_ref=keys.at[there],
            dst_ref=keys.at[there],
            send_sem=pair_send.at[k],
            recv_sem=pair_recv.at[k],
            device_id=sibling,
            device_id_type=MESH,
        )

    def whiten(k, _):
        here = pl.ds(pl.multiple_of(k * 256, 256), 256)
        there = pl.ds(pl.multiple_of(base + k * 256, 256), 256)
        parts = []
        norm = jnp.zeros((256, 1), F32)
        for j in range(4):
            deep = 256 * (j + 1)
            a = received[here, :deep]
            out = slice(256 * j, deep)
            p = dot(a, w_hi[out, :deep], 1, 1) + dot(a, w_lo[out, :deep], 1, 1) - shift[:, out]
            parts.append(p)
            norm = norm + jnp.sum(p * p, axis=1, keepdims=True)
        scale = lax.rsqrt(norm + 1e-06)
        for j in range(4):
            keys[there, 256 * j : 256 * j + 256] = (parts[j] * scale).astype(BF)
        keys[there, width:] = received[here, width:]
        pair_copy(k).start()
        return 0

    chunks = keys_half // 256
    lax.fori_loop(0, chunks, whiten, 0)

    def weights(shape, dim):
        i = lax.broadcasted_iota(jnp.int32, shape, dim)
        w = jnp.where(i == 0, 65536.0, jnp.where(i == 1, 256.0, jnp.where(i == 2, 1.0, 0.0)))
        return w.astype(BF)

    def rank_rows(first):
        here = pl.ds(pl.multiple_of(first, keys_half), keys_half)
        key_rank[:, here] = dot(weights((8, DIGITS), 1), keys[here, width:], 1, 1)

    def pair_wait(k, _):
        pair_copy(k).wait_recv()
        return 0

    rank_rows(base)
    lax.fori_loop(0, chunks, pair_wait, 0)
    rank_rows(keys_half - base)

    def score(k, _):
        here = pl.ds(pl.multiple_of(base + k * 256, 256), 256)
        q = keys[here, :width]
        q_rank = dot(keys[here, width:], weights((DIGITS, BL), 0), 1, 0)

        def part(m, best):
            there = pl.ds(pl.multiple_of(m * 512, 512), 512)
            s = dot(q, keys[there, :width], 1, 1)
            rank = key_rank[0:1, there]
            for n in range(4):
                at = slice(n * BL, (n + 1) * BL)
                best = jnp.maximum(best, jnp.where(rank[:, at] > q_rank, s[:, at], -1.0))
            return best

        best = lax.fori_loop(0, 2 * keys_half // 512, part, jnp.full((256, BL), -1.0, F32))
        top = jnp.broadcast_to(jnp.max(best, axis=1, keepdims=True), (256, BL))
        for h in range(2):
            line = jnp.sum(
                jnp.where(lane == sub, top[h * BL : (h + 1) * BL], 0.0), axis=0, keepdims=True
            )
            ret_out[2 * k + h] = bcast(line)
        return 0

    lax.fori_loop(0, chunks, score, 0)

    def ret_copy(to, at):
        return pltpu.make_async_remote_copy(
            src_ref=ret_out.at[to // 4],
            dst_ref=ret_in.at[chip],
            send_sem=ret_send.at[at],
            recv_sem=ret_recv.at[at],
            device_id=chip_device(to),
            device_id_type=MESH,
        )

    def send_back(d, _):
        ret_copy((chip + d) % CHIPS, d).start()
        return 0

    lax.fori_loop(1, CHIPS, send_back, 0)
    ret_in[chip] = ret_out[chip // 4]

    def come_back(d, _):
        ret_copy((chip + d) % CHIPS, d).wait_recv()
        return 0

    lax.fori_loop(1, CHIPS, come_back, 0)
    table = ret_in[:, 0, :]
    picks = member.astype(F32).astype(BF)
    hi = table.astype(BF)
    rest = table - hi.astype(F32)
    mid = rest.astype(BF)
    low = (rest - mid.astype(F32)).astype(BF)
    mine_of = dot(hi, picks, 0, 0) + (dot(mid, picks, 0, 0) + dot(low, picks, 0, 0))
    at_lane = lax.broadcasted_iota(jnp.int32, (BL, rows), 0) == slot + SEND * (chip % 4)
    out_ref[...] = jnp.sum(jnp.where(at_lane, mine_of, 0.0), axis=0, keepdims=True)

    swap.wait_send()
    for stage in (stage1, stage2, stage3, stage4, stage5):
        for c in stage.values():
            c.wait_send()
    for c in up:
        c.wait_send()

    def left(d, _):
        out_copy((chip + d) % CHIPS, d, chip).wait_send()
        ret_copy((chip + d) % CHIPS, d).wait_send()
        return 0

    lax.fori_loop(1, CHIPS, left, 0)

    def pair_left(k, _):
        pair_copy(k).wait_send()
        return 0

    lax.fori_loop(0, chunks, pair_left, 0)


def per_device(embeddings, clusters, doc_order):
    rows, width = embeddings.shape
    doc_count = rows * lax.axis_size("dp") * lax.axis_size("help")
    slots = CHIPS * SEND
    wide = width + DIGITS
    dma = pltpu.SemaphoreType.DMA
    vmem = pltpu.VMEM
    out = pl.pallas_call(
        lambda *refs: kernel(doc_count, *refs),
        out_shape=jax.ShapeDtypeStruct((1, rows), F32),
        in_specs=[
            pl.BlockSpec(memory_space=pl.ANY),
            pl.BlockSpec(memory_space=pltpu.VMEM),
            pl.BlockSpec(memory_space=pltpu.VMEM),
        ],
        out_specs=pl.BlockSpec(memory_space=pltpu.VMEM),
        scratch_shapes=[
            vmem((rows, width), BF),
            vmem((slots, wide), BF),
            vmem((slots, wide), BF),
            vmem((2 * slots, wide), BF),
            vmem((512, 1152), F32),
            vmem((256, 1152), F32),
            vmem((256, 1152), F32),
            vmem((3, 3, 64, 384), F32),
            vmem((3, 64, 384), F32),
            vmem((3, 3, 16, 384), F32),
            vmem((3, 4, 16, 384), F32),
            vmem((512, 1152), F32),
            vmem((width, width), F32),
            vmem((BL, BL), F32),
            vmem((width, width), BF),
            vmem((width, width), BF),
            vmem((8, 2 * slots), F32),
            vmem((16, 8, BL), F32),
            vmem((CHIPS, 8, BL), F32),
            dma,
            dma,
            dma,
            dma((45,)),
            dma((45,)),
            dma((3,)),
            dma((3,)),
            dma((CHIPS,)),
            dma((CHIPS,)),
            dma((8,)),
            dma((8,)),
            dma((CHIPS,)),
            dma((CHIPS,)),
        ],
        compiler_params=pltpu.CompilerParams(
            collective_id=0, has_side_effects=True, vmem_limit_bytes=56 * 2**20
        ),
    )(embeddings, clusters.reshape(1, rows), doc_order.reshape(1, rows))
    return out.reshape(rows)


def solution(mesh):
    in_specs = (P(("dp", "help"), None), P(("dp", "help")), P(("dp", "help")))
    out_specs = P(("dp", "help"))
    return jax.shard_map(
        per_device, mesh=mesh, in_specs=in_specs, out_specs=out_specs, check_vma=False
    )
```

time: 856 us -> 221 us (0.26)
  other arithmetic: 272 us -> 0 us
  Pallas kernels: 0 us -> 219 us
  waiting for transfers between devices: 206 us -> 0 us
  blocking collectives: 162 us -> 0 us
  matrix products: 105 us -> 0 us
  local copies, waits for them, and re-layouts: 83.9 us -> 1.28 us
  between operations: 19.8 us -> 0.01 us
    another operation x34 -> x0, other arithmetic: 255 us -> none  [the longest x30 170 us: whitening(): factor = jnp.linalg.cholesky(spread + ridge_term * identity)]
    pallas_call x0 -> x1, Pallas kernels: none -> 219 us  [per_device(): pl.pallas_call(lambda *refs: kernel(doc_count, *refs), out_shape=jax.Shap...]
    all_gather x1 -> x0, waiting for transfers between devices: 125 us -> none  [per_device(): key_rows = lax.all_gather(received, 'help', axis=1, tiled=True)]
    all_to_all x3 -> x0, blocking collectives: 82.5 us -> none  [the longest x1 56.8 us: per_device(): lax.all_to_all(outgoing, 'dp', split_axis=1, concat_axis=1, tiled=True)]
    psum x1 -> x0, waiting for transfers between devices: 81.7 us -> none  [per_device(): gram_total, col_sum = lax.psum((gram_part, col_part), ('dp', 'help'))]
    psum x1 -> x0, blocking collectives: 69.5 us -> none  [per_device(): gram_total, col_sum = lax.psum((gram_part, col_part), ('dp', 'help'))]
    another operation x29 -> x0, matrix products: 64.5 us -> none  [the longest x15 38.5 us: whitening(): lax.linalg.triangular_solve(factor, identity, left_side=True, lower=True)]
    dot_general x5 -> x0, matrix products: 40.8 us -> none  [the longest x1 25.4 us: row_best(): jnp.einsum('nqd,nkd->nqk', queries, key_rows, preferred_element_type=jnp....]
  transfers between devices with their start and end apart: 2 -> 0, of which waited for: 2 -> 0; matrix products, arithmetic and copies ran while one was open for 1% -> 0% of each run, Pallas kernels for 0% -> 0%
where the time goes in v1:
time: 221 us; the launch traced here: 220 us
  Pallas kernels  219 us (99%)
    pallas_call x1, Pallas kernels, per_device(): pl.pallas_call(lambda *refs: kernel(doc_count, *refs), out_shape=jax.Shap...  219 us

profile of v1, /device:TPU:1, one launch (start us, length us, event | category | flops | bytes accessed | tf_op | source)
XLA Modules:
  0.0 220.4 jit_solution(10226267745410535502)
XLA Ops:
  0.0 219.1 %shard_map.37 = f32[1,1024]{1,0:T(1,128)} custom-call(bf16[1024,1024]{1,0:T(8,128)(2,1)} %refs_0_.1, s32[1,1024]{1,0:T(1,128)} %bitcast.4, s32[1,1024]{1,0:T(1,128)} %bitcast.5), custom_call_target="tpu_custom_call" | custom-call | tf_op jit(solution)/shard_map/pallas_call | solution.py:549
  219.1 1.3 copy.5
